TPU v7x, 256 devices: a whole 4x4x8 slice. The times are simulated.
256 devices in a mesh: seq: 16 (over z, core), head: 4 (over x), dp: 4 (over y).
Axes of the slice: x: 4, y: 4, z: 8, core: 2. Of those that a mesh axis runs over, the one named last changes fastest.
Arguments:
- self_queries: bfloat16 [4, 2048, 2560], P('dp', ('seq', 'head')), may hold values from -8 to 8
- self_keys: bfloat16 [4, 2048, 2560], P('dp', ('seq', 'head')), may hold values from -4 to 4
- self_values: bfloat16 [4, 2048, 2560], P('dp', ('seq', 'head')), may hold values from -6 to 6
- self_cotangent: bfloat16 [4, 2048, 2560], P('dp', ('seq', 'head')), may hold values from -6 to 6
- text_queries: bfloat16 [4, 4096, 2560], P('dp', 'seq', 'head'), may hold values from -8 to 8
- memory_keys: bfloat16 [4, 2048, 2560], P('dp', 'seq', 'head'), may hold values from -4 to 4
- memory_values: bfloat16 [4, 2048, 2560], P('dp', 'seq', 'head'), may hold values from -6 to 6
- text_cotangent: bfloat16 [4, 4096, 2560], P('dp', 'seq', 'head'), may hold values from -6 to 6
- slopes: float32 [2, 20], P(None, 'head'), may hold values from 0.01 to 0.3
- page_counts: int32 [4, 4], P('dp'), may hold values from 1 to 1024, as said below
- page_cols: int32 [4, 4], P('dp'), may hold values from 4 to 64
- text_page: int32 [4, 4096], P('dp'), may hold values from 0 to 3, as said below
Outputs:
- self_query_grad: bfloat16 [4, 2048, 2560], P('dp', ('seq', 'head'))
- self_key_grad: bfloat16 [4, 2048, 2560], P('dp', ('seq', 'head'))
- self_value_grad: bfloat16 [4, 2048, 2560], P('dp', ('seq', 'head'))
- slope_grad: float32 [2, 20], P(None, 'head')
- text_query_grad: bfloat16 [4, 4096, 2560], P('dp', 'seq', 'head')
- memory_key_grad: bfloat16 [4, 2048, 2560], P('dp', 'seq', 'head')
- memory_value_grad: bfloat16 [4, 2048, 2560], P('dp', 'seq', 'head')
Inputs may be any that keep to these rules, and one draw needn't show every extreme that they name: `page_counts`: each pack's counts sum to 2048; one page of every pack has exactly 1024 patches. `text_page`: never falls along a pack's text rows; every page has at least one text row.
All inputs are finite; a program needn't handle non-finite values.
Results may differ from a plain program's by a relative error of at most 0.006.
Values may be sent and summed in bfloat16 or wider, within the bound.
No kernel may reach another device: no remote copies, remote signals or barrier semaphores. Data moves between devices by JAX's collectives and lax.ppermute only.
A program may use at most 128 MiB of HBM per device.

v0:
```python
import jax
import jax.numpy as jnp
from jax import lax
from jax.sharding import PartitionSpec as P

MASK_FILL = -1e30


def page_layout(counts, widths, patch_total):
    page_ends = jnp.cumsum(counts)
    starts = page_ends - counts
    positions = jnp.arange(patch_total, dtype=jnp.int32)
    page_ids = jnp.sum((positions[:, None] >= page_ends[None, :]).astype(jnp.int32), axis=1)
    one_hot = page_ids[:, None] == jnp.arange(counts.shape[0], dtype=jnp.int32)[None, :]
    page_start = jnp.sum(jnp.where(one_hot, starts[None, :], 0), axis=1)
    page_width = jnp.sum(jnp.where(one_hot, widths[None, :], 0), axis=1)
    offsets = positions - page_start
    return (page_ids, offsets // page_width, offsets % page_width)


def take_rows(vector, row_start, row_count):
    return lax.dynamic_slice_in_dim(vector, row_start, row_count, 0)


def heads_of(matrix, head_count):
    return matrix.reshape(matrix.shape[0], head_count, -1)


def alibi(slopes, query_layout, key_layout):
    row_gap = jnp.abs(query_layout[1][:, None] - key_layout[1][None, :]).astype(jnp.float32)
    col_gap = jnp.abs(query_layout[2][:, None] - key_layout[2][None, :]).astype(jnp.float32)
    same_page = query_layout[0][:, None] == key_layout[0][None, :]
    decay = -(slopes[0][:, None, None] * row_gap[None] + slopes[1][:, None, None] * col_gap[None])
    return (jnp.where(same_page[None], decay, MASK_FILL), row_gap, col_gap)


def query_side(queries, key_rows, value_rows, grad_rows, logit_bias):
    inv_root = queries.shape[2] ** (-0.5)
    scores = (
        jnp.einsum("rhs,khs->hrk", queries, key_rows, preferred_element_type=jnp.float32) * inv_root
        + logit_bias
    )
    row_max = jnp.max(scores, axis=2, keepdims=True)
    weights = jnp.exp(scores - row_max)
    row_total = jnp.sum(weights, axis=2, keepdims=True)
    softmax_w = weights / row_total
    log_total = (row_max + jnp.log(row_total))[:, :, 0]
    grad_probs = jnp.einsum(
        "rhs,khs->hrk", grad_rows, value_rows, preferred_element_type=jnp.float32
    )
    row_delta = jnp.sum(softmax_w * grad_probs, axis=2, keepdims=True)
    grad_scores = softmax_w * (grad_probs - row_delta)
    grad_scores_b = grad_scores.astype(jnp.bfloat16)
    query_grad = (
        jnp.einsum("hrk,khs->rhs", grad_scores_b, key_rows, preferred_element_type=jnp.float32)
        * inv_root
    )
    return (
        query_grad,
        grad_scores,
        grad_scores_b,
        softmax_w.astype(jnp.bfloat16),
        log_total,
        row_delta[:, :, 0],
    )


def key_terms(grad_scores_b, softmax_b, queries, grad_rows, row_count):
    inv_root = queries.shape[3] ** (-0.5)
    key_grad = (
        jnp.einsum("chrk,crhs->khs", grad_scores_b, queries, preferred_element_type=jnp.float32)
        * inv_root
    )
    value_grad = jnp.einsum(
        "chrk,crhs->khs", softmax_b, grad_rows, preferred_element_type=jnp.float32
    )
    return jnp.stack([key_grad.reshape(row_count, -1), value_grad.reshape(row_count, -1)], axis=1)


def local(
    self_queries,
    self_keys,
    self_values,
    self_cotangent,
    text_queries,
    memory_keys,
    memory_values,
    text_cotangent,
    slopes,
    page_counts,
    page_cols,
    text_page,
):
    head_count = slopes.shape[1]
    regrouped = (
        lax.all_to_all(self_queries[0], "head", split_axis=1, concat_axis=0, tiled=True),
        lax.all_to_all(self_keys[0], "head", split_axis=1, concat_axis=0, tiled=True),
        lax.all_to_all(self_values[0], "head", split_axis=1, concat_axis=0, tiled=True),
        lax.all_to_all(self_cotangent[0], "head", split_axis=1, concat_axis=0, tiled=True),
    )
    local_queries, local_keys, local_values, local_grads = regrouped
    patch_rows = local_queries.shape[0]
    all_keys, all_values = (
        lax.all_gather(local_keys, "seq", axis=0, tiled=True),
        lax.all_gather(local_values, "seq", axis=0, tiled=True),
    )
    patch_total = all_keys.shape[0]
    whole_layout = page_layout(page_counts[0], page_cols[0], patch_total)
    own_start = lax.axis_index("seq") * patch_rows
    own_layout = tuple((take_rows(item, own_start, patch_rows) for item in whole_layout))
    self_bias, row_gap, col_gap = alibi(slopes, own_layout, whole_layout)
    query_heads = heads_of(local_queries, head_count)
    grad_heads = heads_of(local_grads, head_count)
    self_dq, self_ds, self_ds_b, self_p_b, self_lse, self_delta = query_side(
        query_heads,
        heads_of(all_keys, head_count),
        heads_of(all_values, head_count),
        grad_heads,
        self_bias,
    )
    slope_local = -jnp.stack(
        [
            jnp.sum(self_ds * row_gap[None], axis=(1, 2)),
            jnp.sum(self_ds * col_gap[None], axis=(1, 2)),
        ]
    )
    self_ds_blocks = self_ds_b[None]
    self_p_blocks = self_p_b[None]
    query_blocks = query_heads[None]
    grad_blocks = grad_heads[None]
    self_pair = lax.psum_scatter(
        key_terms(
            self_ds_blocks,
            self_p_blocks,
            query_blocks,
            grad_blocks,
            patch_rows * lax.axis_size("seq"),
        ),
        "seq",
        scatter_dimension=0,
        tiled=True,
    )
    self_dk = self_pair[:, 0]
    self_dv = self_pair[:, 1]
    restored = (
        lax.all_to_all(
            self_dq.reshape(patch_rows, -1).astype(jnp.bfloat16),
            "head",
            split_axis=0,
            concat_axis=1,
            tiled=True,
        ),
        lax.all_to_all(
            self_dk.astype(jnp.bfloat16), "head", split_axis=0, concat_axis=1, tiled=True
        ),
        lax.all_to_all(
            self_dv.astype(jnp.bfloat16), "head", split_axis=0, concat_axis=1, tiled=True
        ),
    )
    slope_grad = lax.psum(slope_local, ("seq", "dp")) / patch_total
    memory_all_keys, memory_all_values = (
        lax.all_gather(memory_keys[0], "seq", axis=0, tiled=True),
        lax.all_gather(memory_values[0], "seq", axis=0, tiled=True),
    )
    memory_all_key_heads = heads_of(memory_all_keys, head_count)
    memory_all_value_heads = heads_of(memory_all_values, head_count)
    text_rows = text_queries.shape[1]
    text_start = lax.axis_index("seq") * text_rows
    text_ids = text_page[0]
    own_text = take_rows(text_ids, text_start, text_rows)
    text_query_heads = heads_of(text_queries[0], head_count)
    text_grad_heads = heads_of(text_cotangent[0], head_count)
    block_count = text_rows // text_rows
    text_query_blocks = text_query_heads.reshape(block_count, text_rows, head_count, -1)
    text_grad_blocks = text_grad_heads.reshape(block_count, text_rows, head_count, -1)

    def cross_block(inputs):
        block_queries, block_grads, block_pages = inputs
        block_bias = jnp.where(
            block_pages[:, None] == whole_layout[0][None, :], 0.0, MASK_FILL
        ).astype(jnp.float32)[None]
        result = query_side(
            block_queries, memory_all_key_heads, memory_all_value_heads, block_grads, block_bias
        )
        return (result[0], result[2], result[3], result[4], result[5])

    cross_out = lax.map(
        cross_block, (text_query_blocks, text_grad_blocks, own_text.reshape(block_count, text_rows))
    )
    text_dq = cross_out[0].reshape(text_rows, -1)
    text_ds_b = cross_out[1]
    text_p_b = cross_out[2]
    memory_pair = lax.psum_scatter(
        key_terms(
            text_ds_b,
            text_p_b,
            text_query_blocks,
            text_grad_blocks,
            patch_rows * lax.axis_size("seq"),
        ),
        "seq",
        scatter_dimension=0,
        tiled=True,
    )
    memory_dk = memory_pair[:, 0]
    memory_dv = memory_pair[:, 1]
    return (
        restored[0][None],
        restored[1][None],
        restored[2][None],
        slope_grad,
        text_dq.astype(jnp.bfloat16)[None],
        memory_dk.astype(jnp.bfloat16)[None],
        memory_dv.astype(jnp.bfloat16)[None],
    )


def solution(mesh):
    in_specs = (
        P("dp", ("seq", "head"), None),
        P("dp", ("seq", "head"), None),
        P("dp", ("seq", "head"), None),
        P("dp", ("seq", "head"), None),
        P("dp", "seq", "head"),
        P("dp", "seq", "head"),
        P("dp", "seq", "head"),
        P("dp", "seq", "head"),
        P(None, "head"),
        P("dp", None),
        P("dp", None),
        P("dp", None),
    )
    out_specs = (
        P("dp", ("seq", "head"), None),
        P("dp", ("seq", "head"), None),
        P("dp", ("seq", "head"), None),
        P(None, "head"),
        P("dp", "seq", "head"),
        P("dp", "seq", "head"),
        P("dp", "seq", "head"),
    )
    return jax.shard_map(local, mesh=mesh, in_specs=in_specs, out_specs=out_specs, check_vma=False)
```

profile of v0, /device:TPU:2, one launch (start us, length us, event | category | flops | bytes accessed | tf_op | source)
XLA Modules:
  0.0 406.0 jit_solution(9305916653580052399)
XLA Ops:
  7.3 1.0 all_to_all.85
  8.3 10.0 %all_to_all.109 = bf16[32,4,640]{2,0,1:T(8,128)(2,1)} all-to-all(bf16[32,4,640]{2,0,1:T(8,128)(2,1)S(1)} %copy.117), channel_id=1, replica_groups=mesh['seq'=16,'head'=4,'dp'=4] {'head'}, dimensions={1} | all-to-all | bytes 327680 | tf_op jit(solution)/shard_map/all_to_all | solution.py:97
  19.4 9.2 %all_to_all.110 = bf16[32,4,640]{2,0,1:T(8,128)(2,1)} all-to-all(bf16[32,4,640]{2,0,1:T(8,128)(2,1)S(1)} %copy.122), channel_id=1, replica_groups=mesh['seq'=16,'head'=4,'dp'=4] {'head'}, dimensions={1} | all-to-all | bytes 327680 | tf_op jit(solution)/shard_map/all_to_all | solution.py:98
  28.6 1.7 copy.136
  30.4 1.0 all_to_all.82
  32.1 4.7 %all-to-all-start = ((bf16[32,4,640]{2,0,1:T(8,128)(2,1)}), bf16[32,4,640]{2,0,1:T(8,128)(2,1)S(1)}, u32[]{:S(2)}, u32[]{:S(2)}) async-start(bf16[32,4,640]{2,0,1:T(8,128)(2,1)} %copy.116), calls=%async_computation | async-start | bytes 327680 | tf_op jit(solution)/shard_map/all_to_all | solution.py:96
  36.8 1.7 copy.140
  41.4 1.8 abs_convert_fusion
  44.2 4.8 %all-to-all-start.2 = ((bf16[32,4,640]{2,0,1:T(8,128)(2,1)}), bf16[32,4,640]{2,0,1:T(8,128)(2,1)S(1)}, u32[]{:S(2)}, u32[]{:S(2)}) async-start(bf16[32,4,640]{2,0,1:T(8,128)(2,1)} %copy.121), calls=%async_computation.2 | async-start | bytes 327680 | tf_op jit(solution)/shard_map/all_to_all | solution.py:99
  49.4 4.3 %all-to-all-done.2 = bf16[32,4,640]{2,0,1:T(8,128)(2,1)S(1)} async-done(((bf16[32,4,640]{2,0,1:T(8,128)(2,1)}), bf16[32,4,640]{2,0,1:T(8,128)(2,1)S(1)}, u32[]{:S(2)}, u32[]{:S(2)}) %all-to-all-start.2) | async-done | bytes 163872 | tf_op jit(solution)/shard_map/all_to_all | solution.py:99
  54.1 6.2 %all-gather.7.cloned.1.call-done = bf16[2048,640]{1,0:T(8,128)(2,1)} async-done(((bf16[128,640]{1,0:T(8,128)(2,1)}), bf16[2048,640]{1,0:T(8,128)(2,1)}) %all-gather.7.cloned.1.call-update) | async-done | bytes 2621456 | tf_op jit(solution)/shard_map/all_gather | solution.py:104
  60.3 3.0 copy.118
  63.3 37.8 %all-gather.9.cloned.1.call-done = bf16[2048,640]{1,0:T(8,128)(2,1)} async-done(((bf16[128,640]{1,0:T(8,128)(2,1)}), bf16[2048,640]{1,0:T(8,128)(2,1)}) %all-gather.9.cloned.1.call-update) | async-done | bytes 2621456 | tf_op jit(solution)/shard_map/all_gather | solution.py:105
  101.0 4.5 %copy.123 = bf16[2048,640]{0,1:T(8,128)(2,1)} copy(bf16[2048,640]{1,0:T(8,128)(2,1)} %all-gather.9.cloned.1.call-done) | data formatting | bytes 5242880 | tf_op jit(solution)/shard_map/all_gather | solution.py:105
  105.5 3.6 select_add_fusion
  109.1 1.6 fusion.28
  110.7 1.0 copy-done.4
  111.7 1.0 copy-done.7
  112.7 1.3 multiply_reduce_fusion.3
  114.3 2.4 multiply_reduce_fusion.2
  116.7 3.2 convolution_multiply_fusion
  119.8 6.0 %copy.131 = f32[2048,1,640]{2,0,1:T(8,128)} copy(f32[2048,1,640]{0,2,1:T(8,128)} %bitcast.79) | data formatting | bytes 10485760 | tf_op jit(solution)/shard_map/stack;reshape | solution.py:77
  125.8 8.0 %fusion.7 = f32[5,2048,128]{1,2,0:T(8,128)} fusion(bf16[128,5,128]{0,2,1:T(8,128)(2,1)S(1)} %copy.130, f32[5,128]{1,0:T(8,128)S(1)} %get-tuple-element.85, f32[5,128,2048]{2,1,0:T(8,128)} %copy-done.4), kind=kOutput, calls=%fused_computation.22 | convolution fusion | flops 339479168 | bytes 10652160 | tf_op jit(solution)/shard_map/chrk,crhs->khs/dot_general | solution.py:74
  133.7 5.9 %copy.132 = f32[2048,1,640]{2,0,1:T(8,128)} copy(f32[2048,1,640]{0,2,1:T(8,128)} %bitcast.84) | data formatting | bytes 10485760 | tf_op jit(solution)/shard_map/stack;reshape | solution.py:77
  139.6 8.8 %pad_maximum_fusion = f32[2048,2,640]{2,0,1:T(8,128)} fusion(f32[2048,1,640]{2,0,1:T(8,128)} %copy.132, f32[2048,1,640]{2,0,1:T(8,128)} %copy.131), kind=kLoop, calls=%fused_computation.2 | loop fusion | flops 2621440 | bytes 20971520 | tf_op jit(solution)/shard_map/stack | solution.py:77
  149.6 1.1 copy.139
  150.8 1.6 compare_select_fusion
  152.4 9.5 %fusion.29 = (f32[5,256]{1,0:T(8,128)S(1)}, f32[5,256,2048]{2,1,0:T(8,128)}) fusion(f32[256,2048]{1,0:T(8,128)} %compare_select_fusion, bf16[256,5,128]{0,2,1:T(8,128)(2,1)S(1)} %bitcast.87, bf16[2048,5,128]{0,2,1:T(8,128)(2,1)} %bitcast.104), kind=kOutput, calls=%fused_computation.62 | convolution fusion | flops 681576448 | bytes 15537152 | tf_op jit(solution)/shard_map/while/body/eval_jaxpr/sub | solution.py:44
  161.8 27.1 %all-gather.13.cloned.1.call-done = bf16[1,2048,640]{1,2,0:T(8,128)(2,1)} async-done(((bf16[1,128,640]{1,2,0:T(8,128)(2,1)}), bf16[1,2048,640]{1,2,0:T(8,128)(2,1)}) %all-gather.13.cloned.1.call-update) | async-done | bytes 2621456 | tf_op jit(solution)/shard_map/all_gather | solution.py:163
  189.0 6.1 %multiply_reduce_fusion = (f32[5,256]{1,0:T(8,128)S(1)}, f32[5,256,2048]{2,1,0:T(8,128)S(1)}) fusion(f32[5,256,2048]{2,1,0:T(8,128)} %get-tuple-element.90, f32[5,256]{1,0:T(8,128)S(1)} %get-tuple-element.89, bf16[256,5,128]{0,2,1:T(8,128)(2,1)S(1)} %bitcast.96, bf16[2048,5,128]{0,2,1:T(8,128)(2,1)} %bitcast.106), kind=kOutput, calls=%fused_computation.5 | convolution fusion | flops 678951680 | bytes 23930880 | tf_op jit(solution)/shard_map/while/body/eval_jaxpr/rhs,khs->hrk/dot_general | solution.py:48
  195.1 1.1 slice-done.1
  196.8 1.8 multiply_convert_fusion
  198.6 3.9 convolution_multiply_fusion.1
  202.6 5.9 %copy.143 = f32[2048,1,640]{2,0,1:T(8,128)} copy(f32[2048,1,640]{0,2,1:T(8,128)} %bitcast.78) | data formatting | bytes 10485760 | tf_op jit(solution)/shard_map/stack;reshape | solution.py:77
  208.5 7.4 %fusion.3 = f32[5,2048,128]{1,2,0:T(8,128)} fusion(bf16[256,5,128]{0,2,1:T(8,128)(2,1)S(1)} %bitcast.97, f32[5,256,2048]{2,1,0:T(8,128)} %get-tuple-element.90, f32[5,256]{1,0:T(8,128)S(1)} %get-tuple-element.89), kind=kOutput, calls=%fused_computation.9 | convolution fusion | flops 676331520 | bytes 16061440 | tf_op jit(solution)/shard_map/chrk,crhs->khs/dot_general | solution.py:74
  215.9 5.9 %copy.144 = f32[2048,1,640]{2,0,1:T(8,128)} copy(f32[2048,1,640]{0,2,1:T(8,128)} %bitcast.85) | data formatting | bytes 10485760 | tf_op jit(solution)/shard_map/stack;reshape | solution.py:77
  221.9 8.7 %pad_maximum_fusion.1 = f32[2048,2,640]{2,0,1:T(8,128)} fusion(f32[2048,1,640]{2,0,1:T(8,128)} %copy.144, f32[2048,1,640]{2,0,1:T(8,128)} %copy.143), kind=kLoop, calls=%fused_computation.3 | loop fusion | flops 2621440 | bytes 20971520 | tf_op jit(solution)/shard_map/stack | solution.py:77
  230.6 5.3 %fusion.14 = bf16[5,256,128]{1,2,0:T(8,128)(2,1)S(1)} fusion(bf16[5,256,2048]{2,1,0:T(8,128)(2,1)} %copy-done.2, bf16[2048,5,128]{0,2,1:T(8,128)(2,1)} %bitcast.105), kind=kOutput, calls=%fused_computation.31 | convolution fusion | flops 671416320 | bytes 8192000 | tf_op jit(solution)/shard_map/while/body/eval_jaxpr/hrk,khs->rhs/dot_general | solution.py:55
  236.9 129.5 %psum.7 = f32[2,5]{1,0:T(2,128)S(1)} all-reduce(f32[2,5]{1,0:T(2,128)S(1)} %maximum_negate_fusion), channel_id=1, replica_groups=mesh['seq'=16,'head'=4,'dp'=4] {'seq','dp'}, use_global_device_ids=true, to_apply=%region_10.11 | all-reduce | flops 10 | bytes 80 | tf_op jit(solution)/shard_map/psum | solution.py:160
  366.3 2.6 fusion.21
  369.9 4.8 %all-to-all-start.4 = ((bf16[4,32,640]{2,1,0:T(8,128)(2,1)}), bf16[4,32,640]{2,1,0:T(8,128)(2,1)S(1)}, u32[]{:S(2)}, u32[]{:S(2)}) async-start(bf16[4,32,640]{2,1,0:T(8,128)(2,1)} %convert_element_type.95), calls=%async_computation.4 | async-start | bytes 327680 | tf_op jit(solution)/shard_map/all_to_all | solution.py:146
  374.7 1.1 convert.8
  376.6 2.8 all-to-all-done.4
  379.4 4.8 %all-to-all-start.5 = ((bf16[4,32,640]{2,1,0:T(8,128)(2,1)}), bf16[4,32,640]{2,1,0:T(8,128)(2,1)S(1)}, u32[]{:S(2)}, u32[]{:S(2)}) async-start(bf16[4,32,640]{2,1,0:T(8,128)(2,1)} %bitcast.21), calls=%async_computation.6 | async-start | bytes 327680 | tf_op jit(solution)/shard_map/all_to_all | solution.py:153
  385.6 1.1 convert.9
  386.7 2.2 all-to-all-done.5
  388.9 4.8 %all-to-all-start.6 = ((bf16[4,32,640]{2,1,0:T(8,128)(2,1)}), bf16[4,32,640]{2,1,0:T(8,128)(2,1)S(1)}, u32[]{:S(2)}, u32[]{:S(2)}) async-start(bf16[4,32,640]{2,1,0:T(8,128)(2,1)} %bitcast.23), calls=%async_computation.7 | async-start | bytes 327680 | tf_op jit(solution)/shard_map/all_to_all | solution.py:156
  395.2 3.1 all-to-all-done.6
  (77 shorter events, 15.1 us)
Async XLA Ops:
  7.2 143.6 %copy-start = (s32[1,4096]{1,0:T(1,128)S(1)}, s32[1,4096]{1,0:T(1,128)}, u32[]{:S(2)}) copy-start(s32[1,4096]{1,0:T(1,128)} %param.23) | copy-start | bytes 49156
  7.2 36.3 %copy-start.9 = (bf16[1,32,2560]{2,1,0:T(8,128)(2,1)S(1)}, bf16[1,32,2560]{2,1,0:T(8,128)(2,1)}, u32[]{:S(2)}) copy-start(bf16[1,32,2560]{2,1,0:T(8,128)(2,1)} %param.15) | copy-start | bytes 491524
  7.2 41.8 %copy-start.10 = (f32[2,5]{1,0:T(2,128)S(1)}, f32[2,5]{1,0:T(2,128)}, u32[]{:S(2)}) copy-start(f32[2,5]{1,0:T(2,128)} %param.20) | copy-start | bytes 124
  7.2 53.1 %all-gather.7.cloned.1.call-start = ((), (), s32[]{:S(2)}) async-start(), calls=%async_computation.9 | async-start | bytes 2785280 | tf_op jit(solution)/shard_map/all_gather | solution.py:104
  18.3 82.7 %all-gather.9.cloned.1.call-start = ((), (), s32[]{:S(2)}) async-start(), calls=%async_computation.10 | async-start | bytes 2785280 | tf_op jit(solution)/shard_map/all_gather | solution.py:105
  28.6 123.8 %all-gather.11.cloned.1.call-start = ((), (), s32[]{:S(2)}) async-start(), calls=%async_computation.13 | async-start | bytes 2785280 | tf_op jit(solution)/shard_map/all_gather | solution.py:162
  32.1 12.1 %all-to-all-start = ((bf16[32,4,640]{2,0,1:T(8,128)(2,1)}), bf16[32,4,640]{2,0,1:T(8,128)(2,1)S(1)}, u32[]{:S(2)}, u32[]{:S(2)}) async-start(bf16[32,4,640]{2,0,1:T(8,128)(2,1)} %copy.116), calls=%async_computation | async-start | bytes 327680 | tf_op jit(solution)/shard_map/all_to_all | solution.py:96
  36.8 152.2 %all-gather.13.cloned.1.call-start = ((), (), s32[]{:S(2)}) async-start(), calls=%async_computation.14 | async-start | bytes 2785280 | tf_op jit(solution)/shard_map/all_gather | solution.py:163
  44.2 9.5 %all-to-all-start.2 = ((bf16[32,4,640]{2,0,1:T(8,128)(2,1)}), bf16[32,4,640]{2,0,1:T(8,128)(2,1)S(1)}, u32[]{:S(2)}, u32[]{:S(2)}) async-start(bf16[32,4,640]{2,0,1:T(8,128)(2,1)} %copy.121), calls=%async_computation.2 | async-start | bytes 327680 | tf_op jit(solution)/shard_map/all_to_all | solution.py:99
  49.0 325.7 %reduce-scatter.3.cloned.1.call-start = ((), (), s32[]{:S(2)}) async-start(), calls=%async_computation.11 | async-start | bytes 11141120 | tf_op jit(solution)/shard_map/reduce_scatter | solution.py:131
  63.3 45.8 %copy-start.3 = (bf16[2048,640]{0,1:T(8,128)(2,1)}, bf16[2048,640]{0,1:T(8,128)(2,1)S(1)}, u32[]{:S(2)}) copy-start(bf16[2048,640]{0,1:T(8,128)(2,1)S(1)} %copy.118) | copy-start | bytes 7864324
  109.1 2.7 copy-start.4
  109.1 3.6 copy-start.7
  112.7 1.3 copy-start.5
  112.7 1.6 copy-start.6
  148.4 1.0 copy-start.8
  148.5 237.1 %reduce-scatter.5.cloned.1.call-start = ((), (), s32[]{:S(2)}) async-start(), calls=%async_computation.12 | async-start | bytes 11141120 | tf_op jit(solution)/shard_map/reduce_scatter | solution.py:193
  189.0 6.1 %slice-start = ((s8[10485760]{0:T(1024)(128)(4,1)}), s8[4194304]{0:T(1024)(128)(4,1)S(1)}, s32[]{:S(2)}) async-start(s8[10485760]{0:T(1024)(128)(4,1)} %bitcast.80), calls=%async_computation.15 | async-start | bytes 8388608
  189.0 7.3 %slice-start.1 = ((s8[10485760]{0:T(1024)(128)(4,1)}), s8[4194304]{0:T(1024)(128)(4,1)S(1)}, s32[]{:S(2)}) async-start(s8[10485760]{0:T(1024)(128)(4,1)} %bitcast.80), calls=%async_computation.16 | async-start | bytes 8388608
  189.0 7.9 %slice-start.2 = ((s8[10485760]{0:T(1024)(128)(4,1)}), s8[2097152]{0:T(1024)(128)(4,1)S(1)}, s32[]{:S(2)}) async-start(s8[10485760]{0:T(1024)(128)(4,1)} %bitcast.80), calls=%async_computation.17 | async-start | bytes 4194304
  198.6 4.0 copy-start.2
  236.9 162.3 %copy-start.1 = (s32[1,4096]{1,0:T(1,128)S(1)}, s32[1,4096]{1,0:T(1,128)}, u32[]{:S(2)}) copy-start(s32[1,4096]{1,0:T(1,128)} %param.23) | copy-start | bytes 49156
  369.9 9.5 %all-to-all-start.4 = ((bf16[4,32,640]{2,1,0:T(8,128)(2,1)}), bf16[4,32,640]{2,1,0:T(8,128)(2,1)S(1)}, u32[]{:S(2)}, u32[]{:S(2)}) async-start(bf16[4,32,640]{2,1,0:T(8,128)(2,1)} %convert_element_type.95), calls=%async_computation.4 | async-start | bytes 327680 | tf_op jit(solution)/shard_map/all_to_all | solution.py:146
  379.4 9.5 %all-to-all-start.5 = ((bf16[4,32,640]{2,1,0:T(8,128)(2,1)}), bf16[4,32,640]{2,1,0:T(8,128)(2,1)S(1)}, u32[]{:S(2)}, u32[]{:S(2)}) async-start(bf16[4,32,640]{2,1,0:T(8,128)(2,1)} %bitcast.21), calls=%async_computation.6 | async-start | bytes 327680 | tf_op jit(solution)/shard_map/all_to_all | solution.py:153
  388.9 9.5 %all-to-all-start.6 = ((bf16[4,32,640]{2,1,0:T(8,128)(2,1)}), bf16[4,32,640]{2,1,0:T(8,128)(2,1)S(1)}, u32[]{:S(2)}, u32[]{:S(2)}) async-start(bf16[4,32,640]{2,1,0:T(8,128)(2,1)} %bitcast.23), calls=%async_computation.7 | async-start | bytes 327680 | tf_op jit(solution)/shard_map/all_to_all | solution.py:156
Sparse Core Ops, SparseCore 0:
  18.5 41.7 all-gather.6
  62.1 38.8 all-gather.8
  103.4 41.4 all-gather.10
  147.0 41.9 all-gather.12
  191.4 73.8 reduce-scatter.2
  267.7 74.0 reduce-scatter.4
where the time goes:
time: 408 us; the launch traced here: 406 us
  blocking collectives  149 us (37%)
  waiting for transfers between devices  83.5 us (20%)
  local copies, waits for them, and re-layouts  52.1 us (13%)
  matrix products  50.7 us (12%)
  other arithmetic  32.3 us (8%)
  starting transfers between devices  24.2 us (6%)
  between operations  14.4 us (4%)
    psum x1, blocking collectives, local(): slope_grad = lax.psum(slope_local, ('seq', 'dp')) / patch_total  129 us
    all_gather x1, waiting for transfers between devices, local(): lax.all_gather(local_values, 'seq', axis=0, tiled=True)  37.8 us
    all_gather x1, waiting for transfers between devices, local(): lax.all_gather(memory_values[0], 'seq', axis=0, tiled=True)  27.1 us
    another operation x4, local copies, waits for them, and re-layouts, key_terms(): jnp.stack([key_grad.reshape(row_count, -1), value_grad.reshape(row_count,...  23.7 us
    another operation x2, other arithmetic, key_terms(): jnp.stack([key_grad.reshape(row_count, -1), value_grad.reshape(row_count,...  17.5 us
    dot_general x2, matrix products, key_terms(): jnp.einsum('chrk,crhs->khs', softmax_b, grad_rows, preferred_element_type...  15.4 us
    unnamed x33, local copies, waits for them, and re-layouts  10.6 us
    all_to_all x1, blocking collectives, local(): lax.all_to_all(self_keys[0], 'head', split_axis=1, concat_axis=0, tiled=T...  10 us
  transfers between devices with their start and end apart: 11, of which 7 were waited for; matrix products, arithmetic and copies ran while one was open for 31% of the time, Pallas kernels for 0%

commit v1 on v0

--- a/solution.py
+++ b/solution.py
@@ -2,6 +2,7 @@
 import jax.numpy as jnp
 from jax import lax
 from jax.sharding import PartitionSpec as P
+from jax.lax import psum
 
 MASK_FILL = -1e30
 
@@ -157,7 +158,11 @@
             self_dv.astype(jnp.bfloat16), "head", split_axis=0, concat_axis=1, tiled=True
         ),
     )
-    slope_grad = lax.psum(slope_local, ("seq", "dp")) / patch_total
+
+    def feed_the_record(slab_in, a_name, lane_axis):
+        return psum(psum(slab_in, axis_name=a_name), axis_name=lane_axis)
+
+    slope_grad = feed_the_record(slope_local, "seq", "dp") / patch_total
     memory_all_keys, memory_all_values = (
         lax.all_gather(memory_keys[0], "seq", axis=0, tiled=True),
         lax.all_gather(memory_values[0], "seq", axis=0, tiled=True),

time: 408 us -> 362 us (0.89)
  blocking collectives: 149 us -> 55.9 us
  waiting for transfers between devices: 83.5 us -> 130 us
    psum x1 -> x2, blocking collectives: 129 us -> 36.7 us  [feed_the_record(): return psum(psum(slab_in, axis_name=a_name), axis_name=lane_axis)]
    reduce_scatter x1, waiting for transfers between devices: 0.01 us -> 48.7 us  [local(): lax.psum_scatter(key_terms(text_ds_b, text_p_b, text_query_blocks, text_g...]
  transfers between devices with their start and end apart: 11 -> 11, of which waited for: 7 -> 7; matrix products, arithmetic and copies ran while one was open for 31% -> 35% of each run, Pallas kernels for 0% -> 0%
where the time goes in v1:
time: 362 us; the launch traced here: 360 us
  waiting for transfers between devices  130 us (36%)
  blocking collectives  55.9 us (15%)
  local copies, waits for them, and re-layouts  52.2 us (14%)
  matrix products  50.7 us (14%)
  other arithmetic  32.3 us (9%)
  starting transfers between devices  24.3 us (7%)
  between operations  14.4 us (4%)
    reduce_scatter x1, waiting for transfers between devices, local(): lax.psum_scatter(key_terms(text_ds_b, text_p_b, text_query_blocks, text_g...  48.7 us
    all_gather x1, waiting for transfers between devices, local(): lax.all_gather(local_values, 'seq', axis=0, tiled=True)  37.8 us
    psum x2, blocking collectives, feed_the_record(): return psum(psum(slab_in, axis_name=a_name), axis_name=lane_axis)  36.7 us
    all_gather x1, waiting for transfers between devices, local(): lax.all_gather(memory_values[0], 'seq', axis=0, tiled=True)  27.1 us
    another operation x4, local copies, waits for them, and re-layouts, key_terms(): jnp.stack([key_grad.reshape(row_count, -1), value_grad.reshape(row_count,...  23.7 us
    another operation x2, other arithmetic, key_terms(): jnp.stack([key_grad.reshape(row_count, -1), value_grad.reshape(row_count,...  17.5 us
    dot_general x2, matrix products, key_terms(): jnp.einsum('chrk,crhs->khs', softmax_b, grad_rows, preferred_element_type...  15.4 us
    unnamed x33, local copies, waits for them, and re-layouts  10.6 us
  transfers between devices with their start and end apart: 11, of which 7 were waited for; matrix products, arithmetic and copies ran while one was open for 35% of the time, Pallas kernels for 0%

profile of v1, /device:TPU:2, one launch (start us, length us, event | category | flops | bytes accessed | tf_op | source)
XLA Modules:
  0.0 359.8 jit_solution(12420908455035417592)
XLA Ops:
  7.3 1.0 all_to_all.85
  8.3 10.0 %all_to_all.109 = bf16[32,4,640]{2,0,1:T(8,128)(2,1)} all-to-all(bf16[32,4,640]{2,0,1:T(8,128)(2,1)S(1)} %copy.117), channel_id=1, replica_groups=mesh['seq'=16,'head'=4,'dp'=4] {'head'}, dimensions={1} | all-to-all | bytes 327680 | tf_op jit(solution)/shard_map/all_to_all | solution.py:98
  19.4 9.2 %all_to_all.110 = bf16[32,4,640]{2,0,1:T(8,128)(2,1)} all-to-all(bf16[32,4,640]{2,0,1:T(8,128)(2,1)S(1)} %copy.122), channel_id=1, replica_groups=mesh['seq'=16,'head'=4,'dp'=4] {'head'}, dimensions={1} | all-to-all | bytes 327680 | tf_op jit(solution)/shard_map/all_to_all | solution.py:99
  28.6 1.7 copy.136
  30.4 1.0 all_to_all.82
  32.1 4.7 %all-to-all-start = ((bf16[32,4,640]{2,0,1:T(8,128)(2,1)}), bf16[32,4,640]{2,0,1:T(8,128)(2,1)S(1)}, u32[]{:S(2)}, u32[]{:S(2)}) async-start(bf16[32,4,640]{2,0,1:T(8,128)(2,1)} %copy.116), calls=%async_computation | async-start | bytes 327680 | tf_op jit(solution)/shard_map/all_to_all | solution.py:97
  36.8 1.7 copy.140
  41.4 1.8 abs_convert_fusion
  44.2 4.8 %all-to-all-start.2 = ((bf16[32,4,640]{2,0,1:T(8,128)(2,1)}), bf16[32,4,640]{2,0,1:T(8,128)(2,1)S(1)}, u32[]{:S(2)}, u32[]{:S(2)}) async-start(bf16[32,4,640]{2,0,1:T(8,128)(2,1)} %copy.121), calls=%async_computation.2 | async-start | bytes 327680 | tf_op jit(solution)/shard_map/all_to_all | solution.py:100
  49.4 4.3 %all-to-all-done.2 = bf16[32,4,640]{2,0,1:T(8,128)(2,1)S(1)} async-done(((bf16[32,4,640]{2,0,1:T(8,128)(2,1)}), bf16[32,4,640]{2,0,1:T(8,128)(2,1)S(1)}, u32[]{:S(2)}, u32[]{:S(2)}) %all-to-all-start.2) | async-done | bytes 163872 | tf_op jit(solution)/shard_map/all_to_all | solution.py:100
  54.1 6.2 %all-gather.7.cloned.1.call-done = bf16[2048,640]{1,0:T(8,128)(2,1)} async-done(((bf16[128,640]{1,0:T(8,128)(2,1)}), bf16[2048,640]{1,0:T(8,128)(2,1)}) %all-gather.7.cloned.1.call-update) | async-done | bytes 2621456 | tf_op jit(solution)/shard_map/all_gather | solution.py:105
  60.3 3.0 copy.118
  63.3 37.8 %all-gather.9.cloned.1.call-done = bf16[2048,640]{1,0:T(8,128)(2,1)} async-done(((bf16[128,640]{1,0:T(8,128)(2,1)}), bf16[2048,640]{1,0:T(8,128)(2,1)}) %all-gather.9.cloned.1.call-update) | async-done | bytes 2621456 | tf_op jit(solution)/shard_map/all_gather | solution.py:106
  101.0 4.5 %copy.123 = bf16[2048,640]{0,1:T(8,128)(2,1)} copy(bf16[2048,640]{1,0:T(8,128)(2,1)} %all-gather.9.cloned.1.call-done) | data formatting | bytes 5242880 | tf_op jit(solution)/shard_map/all_gather | solution.py:106
  105.5 3.6 select_add_fusion
  109.2 1.6 fusion.28
  110.8 1.0 copy-done.4
  112.8 1.3 multiply_reduce_fusion.3
  114.3 2.4 multiply_reduce_fusion.2
  116.7 3.2 convolution_multiply_fusion
  119.9 6.0 %copy.131 = f32[2048,1,640]{2,0,1:T(8,128)} copy(f32[2048,1,640]{0,2,1:T(8,128)} %bitcast.79) | data formatting | bytes 10485760 | tf_op jit(solution)/shard_map/stack;reshape | solution.py:78
  125.9 8.0 %fusion.7 = f32[5,2048,128]{1,2,0:T(8,128)} fusion(bf16[128,5,128]{0,2,1:T(8,128)(2,1)S(1)} %copy.130, f32[5,128]{1,0:T(8,128)S(1)} %get-tuple-element.85, f32[5,128,2048]{2,1,0:T(8,128)} %copy-done.4), kind=kOutput, calls=%fused_computation.22 | convolution fusion | flops 339479168 | bytes 10652160 | tf_op jit(solution)/shard_map/chrk,crhs->khs/dot_general | solution.py:75
  133.8 5.9 %copy.132 = f32[2048,1,640]{2,0,1:T(8,128)} copy(f32[2048,1,640]{0,2,1:T(8,128)} %bitcast.84) | data formatting | bytes 10485760 | tf_op jit(solution)/shard_map/stack;reshape | solution.py:78
  139.7 8.8 %pad_maximum_fusion = f32[2048,2,640]{2,0,1:T(8,128)} fusion(f32[2048,1,640]{2,0,1:T(8,128)} %copy.132, f32[2048,1,640]{2,0,1:T(8,128)} %copy.131), kind=kLoop, calls=%fused_computation.2 | loop fusion | flops 2621440 | bytes 20971520 | tf_op jit(solution)/shard_map/stack | solution.py:78
  149.7 1.1 copy.139
  150.8 1.6 compare_select_fusion
  152.4 9.5 %fusion.29 = (f32[5,256]{1,0:T(8,128)S(1)}, f32[5,256,2048]{2,1,0:T(8,128)}) fusion(f32[256,2048]{1,0:T(8,128)} %compare_select_fusion, bf16[256,5,128]{0,2,1:T(8,128)(2,1)S(1)} %bitcast.87, bf16[2048,5,128]{0,2,1:T(8,128)(2,1)} %bitcast.104), kind=kOutput, calls=%fused_computation.62 | convolution fusion | flops 681576448 | bytes 15537152 | tf_op jit(solution)/shard_map/while/body/eval_jaxpr/sub | solution.py:45
  161.9 27.1 %all-gather.13.cloned.1.call-done = bf16[1,2048,640]{1,2,0:T(8,128)(2,1)} async-done(((bf16[1,128,640]{1,2,0:T(8,128)(2,1)}), bf16[1,2048,640]{1,2,0:T(8,128)(2,1)}) %all-gather.13.cloned.1.call-update) | async-done | bytes 2621456 | tf_op jit(solution)/shard_map/all_gather | solution.py:168
  189.0 6.1 %multiply_reduce_fusion = (f32[5,256]{1,0:T(8,128)S(1)}, f32[5,256,2048]{2,1,0:T(8,128)S(1)}) fusion(f32[5,256,2048]{2,1,0:T(8,128)} %get-tuple-element.90, f32[5,256]{1,0:T(8,128)S(1)} %get-tuple-element.89, bf16[256,5,128]{0,2,1:T(8,128)(2,1)S(1)} %bitcast.96, bf16[2048,5,128]{0,2,1:T(8,128)(2,1)} %bitcast.106), kind=kOutput, calls=%fused_computation.5 | convolution fusion | flops 678951680 | bytes 23930880 | tf_op jit(solution)/shard_map/while/body/eval_jaxpr/rhs,khs->hrk/dot_general | solution.py:49
  195.1 1.1 slice-done.1
  196.8 1.8 multiply_convert_fusion
  198.6 3.9 %convolution_multiply_fusion.1 = f32[5,2048,128]{1,2,0:T(8,128)} fusion(bf16[256,5,128]{0,2,1:T(8,128)(2,1)S(1)} %bitcast.88, bf16[5,256,2048]{2,1,0:T(8,128)(2,1)S(1)} %multiply_convert_fusion), kind=kOutput, calls=%fused_computation.21 | convolution fusion | flops 672399360 | bytes 10813440 | tf_op jit(solution)/shard_map/chrk,crhs->khs/dot_general | solution.py:72
  202.6 5.9 %copy.143 = f32[2048,1,640]{2,0,1:T(8,128)} copy(f32[2048,1,640]{0,2,1:T(8,128)} %bitcast.78) | data formatting | bytes 10485760 | tf_op jit(solution)/shard_map/stack;reshape | solution.py:78
  208.5 7.4 %fusion.3 = f32[5,2048,128]{1,2,0:T(8,128)} fusion(bf16[256,5,128]{0,2,1:T(8,128)(2,1)S(1)} %bitcast.97, f32[5,256,2048]{2,1,0:T(8,128)} %get-tuple-element.90, f32[5,256]{1,0:T(8,128)S(1)} %get-tuple-element.89), kind=kOutput, calls=%fused_computation.9 | convolution fusion | flops 676331520 | bytes 16061440 | tf_op jit(solution)/shard_map/chrk,crhs->khs/dot_general | solution.py:75
  215.9 5.9 %copy.144 = f32[2048,1,640]{2,0,1:T(8,128)} copy(f32[2048,1,640]{0,2,1:T(8,128)} %bitcast.85) | data formatting | bytes 10485760 | tf_op jit(solution)/shard_map/stack;reshape | solution.py:78
  221.9 8.7 %pad_maximum_fusion.1 = f32[2048,2,640]{2,0,1:T(8,128)} fusion(f32[2048,1,640]{2,0,1:T(8,128)} %copy.144, f32[2048,1,640]{2,0,1:T(8,128)} %copy.143), kind=kLoop, calls=%fused_computation.3 | loop fusion | flops 2621440 | bytes 20971520 | tf_op jit(solution)/shard_map/stack | solution.py:78
  230.6 5.3 %fusion.14 = bf16[5,256,128]{1,2,0:T(8,128)(2,1)S(1)} fusion(bf16[5,256,2048]{2,1,0:T(8,128)(2,1)} %copy-done.2, bf16[2048,5,128]{0,2,1:T(8,128)(2,1)} %bitcast.105), kind=kOutput, calls=%fused_computation.31 | convolution fusion | flops 671416320 | bytes 8192000 | tf_op jit(solution)/shard_map/while/body/eval_jaxpr/hrk,khs->rhs/dot_general | solution.py:56
  235.9 26.1 %psum.14 = f32[2,5]{1,0:T(2,128)S(1)} all-reduce(f32[2,5]{1,0:T(2,128)S(1)} %maximum_negate_fusion), channel_id=1, replica_groups=mesh['seq'=16,'head'=4,'dp'=4] {'seq'}, use_global_device_ids=true, to_apply=%region_10.11 | all-reduce | flops 10 | bytes 80 | tf_op jit(solution)/shard_map/psum | solution.py:163
  263.0 10.6 %psum.15 = f32[2,5]{1,0:T(2,128)S(1)} all-reduce(f32[2,5]{1,0:T(2,128)S(1)} %psum.14), channel_id=1, replica_groups=mesh['seq'=16,'head'=4,'dp'=4] {'dp'}, use_global_device_ids=true, to_apply=%region_11.12 | all-reduce | flops 10 | bytes 80 | tf_op jit(solution)/shard_map/psum | solution.py:163
  273.5 2.6 fusion.21
  277.1 4.8 %all-to-all-start.4 = ((bf16[4,32,640]{2,1,0:T(8,128)(2,1)}), bf16[4,32,640]{2,1,0:T(8,128)(2,1)S(1)}, u32[]{:S(2)}, u32[]{:S(2)}) async-start(bf16[4,32,640]{2,1,0:T(8,128)(2,1)} %convert_element_type.95), calls=%async_computation.4 | async-start | bytes 327680 | tf_op jit(solution)/shard_map/all_to_all | solution.py:147
  281.9 1.1 convert.8
  283.8 2.8 all-to-all-done.4
  286.6 4.8 %all-to-all-start.5 = ((bf16[4,32,640]{2,1,0:T(8,128)(2,1)}), bf16[4,32,640]{2,1,0:T(8,128)(2,1)S(1)}, u32[]{:S(2)}, u32[]{:S(2)}) async-start(bf16[4,32,640]{2,1,0:T(8,128)(2,1)} %bitcast.21), calls=%async_computation.6 | async-start | bytes 327680 | tf_op jit(solution)/shard_map/all_to_all | solution.py:154
  292.8 48.7 %reduce-scatter.5.cloned.1.call-done = f32[128,2,640]{2,0,1:T(8,128)} async-done(((f32[2048,2,640]{2,0,1:T(8,128)}), f32[128,2,640]{2,0,1:T(8,128)}) %reduce-scatter.5.cloned.1.call-update) | async-done | bytes 655376 | tf_op jit(solution)/shard_map/reduce_scatter | solution.py:198
  341.5 1.1 convert.9
  342.6 4.8 %all-to-all-start.6 = ((bf16[4,32,640]{2,1,0:T(8,128)(2,1)}), bf16[4,32,640]{2,1,0:T(8,128)(2,1)S(1)}, u32[]{:S(2)}, u32[]{:S(2)}) async-start(bf16[4,32,640]{2,1,0:T(8,128)(2,1)} %bitcast.23), calls=%async_computation.7 | async-start | bytes 327680 | tf_op jit(solution)/shard_map/all_to_all | solution.py:157
  349.0 3.1 all-to-all-done.6
  (78 shorter events, 16.0 us)
Async XLA Ops:
  7.2 143.6 %copy-start = (s32[1,4096]{1,0:T(1,128)S(1)}, s32[1,4096]{1,0:T(1,128)}, u32[]{:S(2)}) copy-start(s32[1,4096]{1,0:T(1,128)} %param.23) | copy-start | bytes 49156
  7.2 36.2 %copy-start.9 = (bf16[1,32,2560]{2,1,0:T(8,128)(2,1)S(1)}, bf16[1,32,2560]{2,1,0:T(8,128)(2,1)}, u32[]{:S(2)}) copy-start(bf16[1,32,2560]{2,1,0:T(8,128)(2,1)} %param.15) | copy-start | bytes 491524
  7.2 41.8 %copy-start.10 = (f32[2,5]{1,0:T(2,128)S(1)}, f32[2,5]{1,0:T(2,128)}, u32[]{:S(2)}) copy-start(f32[2,5]{1,0:T(2,128)} %param.20) | copy-start | bytes 124
  7.2 53.1 %all-gather.7.cloned.1.call-start = ((), (), s32[]{:S(2)}) async-start(), calls=%async_computation.9 | async-start | bytes 2785280 | tf_op jit(solution)/shard_map/all_gather | solution.py:105
  18.3 82.7 %all-gather.9.cloned.1.call-start = ((), (), s32[]{:S(2)}) async-start(), calls=%async_computation.10 | async-start | bytes 2785280 | tf_op jit(solution)/shard_map/all_gather | solution.py:106
  28.6 123.8 %all-gather.11.cloned.1.call-start = ((), (), s32[]{:S(2)}) async-start(), calls=%async_computation.13 | async-start | bytes 2785280 | tf_op jit(solution)/shard_map/all_gather | solution.py:167
  32.1 12.1 %all-to-all-start = ((bf16[32,4,640]{2,0,1:T(8,128)(2,1)}), bf16[32,4,640]{2,0,1:T(8,128)(2,1)S(1)}, u32[]{:S(2)}, u32[]{:S(2)}) async-start(bf16[32,4,640]{2,0,1:T(8,128)(2,1)} %copy.116), calls=%async_computation | async-start | bytes 327680 | tf_op jit(solution)/shard_map/all_to_all | solution.py:97
  36.8 152.1 %all-gather.13.cloned.1.call-start = ((), (), s32[]{:S(2)}) async-start(), calls=%async_computation.14 | async-start | bytes 2785280 | tf_op jit(solution)/shard_map/all_gather | solution.py:168
  44.2 9.5 %all-to-all-start.2 = ((bf16[32,4,640]{2,0,1:T(8,128)(2,1)}), bf16[32,4,640]{2,0,1:T(8,128)(2,1)S(1)}, u32[]{:S(2)}, u32[]{:S(2)}) async-start(bf16[32,4,640]{2,0,1:T(8,128)(2,1)} %copy.121), calls=%async_computation.2 | async-start | bytes 327680 | tf_op jit(solution)/shard_map/all_to_all | solution.py:100
  49.0 233.0 %reduce-scatter.3.cloned.1.call-start = ((), (), s32[]{:S(2)}) async-start(), calls=%async_computation.11 | async-start | bytes 11141120 | tf_op jit(solution)/shard_map/reduce_scatter | solution.py:132
  63.3 45.9 %copy-start.3 = (bf16[2048,640]{0,1:T(8,128)(2,1)}, bf16[2048,640]{0,1:T(8,128)(2,1)S(1)}, u32[]{:S(2)}) copy-start(bf16[2048,640]{0,1:T(8,128)(2,1)S(1)} %copy.118) | copy-start | bytes 7864324
  109.1 2.7 copy-start.4
  109.1 3.6 %copy-start.7 = (bf16[2048,640]{0,1:T(8,128)(2,1)S(1)}, bf16[2048,640]{0,1:T(8,128)(2,1)}, u32[]{:S(2)}) copy-start(bf16[2048,640]{0,1:T(8,128)(2,1)} %copy.123) | copy-start | bytes 7864324
  112.8 1.3 copy-start.5
  112.8 1.6 copy-start.6
  148.5 1.0 copy-start.8
  148.5 193.0 %reduce-scatter.5.cloned.1.call-start = ((), (), s32[]{:S(2)}) async-start(), calls=%async_computation.12 | async-start | bytes 11141120 | tf_op jit(solution)/shard_map/reduce_scatter | solution.py:198
  189.0 6.1 %slice-start = ((s8[10485760]{0:T(1024)(128)(4,1)}), s8[4194304]{0:T(1024)(128)(4,1)S(1)}, s32[]{:S(2)}) async-start(s8[10485760]{0:T(1024)(128)(4,1)} %bitcast.80), calls=%async_computation.15 | async-start | bytes 8388608
  189.0 7.3 %slice-start.1 = ((s8[10485760]{0:T(1024)(128)(4,1)}), s8[4194304]{0:T(1024)(128)(4,1)S(1)}, s32[]{:S(2)}) async-start(s8[10485760]{0:T(1024)(128)(4,1)} %bitcast.80), calls=%async_computation.16 | async-start | bytes 8388608
  189.0 7.9 %slice-start.2 = ((s8[10485760]{0:T(1024)(128)(4,1)}), s8[2097152]{0:T(1024)(128)(4,1)S(1)}, s32[]{:S(2)}) async-start(s8[10485760]{0:T(1024)(128)(4,1)} %bitcast.80), calls=%async_computation.17 | async-start | bytes 4194304
  198.6 4.0 %copy-start.2 = (bf16[5,256,2048]{2,1,0:T(8,128)(2,1)}, bf16[5,256,2048]{2,1,0:T(8,128)(2,1)S(1)}, u32[]{:S(2)}) copy-start(bf16[5,256,2048]{2,1,0:T(8,128)(2,1)S(1)} %multiply_convert_fusion) | copy-start | bytes 15728644
  263.0 90.0 %copy-start.1 = (s32[1,4096]{1,0:T(1,128)S(1)}, s32[1,4096]{1,0:T(1,128)}, u32[]{:S(2)}) copy-start(s32[1,4096]{1,0:T(1,128)} %param.23) | copy-start | bytes 49156
  277.1 9.5 %all-to-all-start.4 = ((bf16[4,32,640]{2,1,0:T(8,128)(2,1)}), bf16[4,32,640]{2,1,0:T(8,128)(2,1)S(1)}, u32[]{:S(2)}, u32[]{:S(2)}) async-start(bf16[4,32,640]{2,1,0:T(8,128)(2,1)} %convert_element_type.95), calls=%async_computation.4 | async-start | bytes 327680 | tf_op jit(solution)/shard_map/all_to_all | solution.py:147
  286.6 56.0 %all-to-all-start.5 = ((bf16[4,32,640]{2,1,0:T(8,128)(2,1)}), bf16[4,32,640]{2,1,0:T(8,128)(2,1)S(1)}, u32[]{:S(2)}, u32[]{:S(2)}) async-start(bf16[4,32,640]{2,1,0:T(8,128)(2,1)} %bitcast.21), calls=%async_computation.6 | async-start | bytes 327680 | tf_op jit(solution)/shard_map/all_to_all | solution.py:154
  342.6 9.5 %all-to-all-start.6 = ((bf16[4,32,640]{2,1,0:T(8,128)(2,1)}), bf16[4,32,640]{2,1,0:T(8,128)(2,1)S(1)}, u32[]{:S(2)}, u32[]{:S(2)}) async-start(bf16[4,32,640]{2,1,0:T(8,128)(2,1)} %bitcast.23), calls=%async_computation.7 | async-start | bytes 327680 | tf_op jit(solution)/shard_map/all_to_all | solution.py:157
Sparse Core Ops, SparseCore 0:
  18.4 41.7 all-gather.6
  62.1 38.8 all-gather.8
  103.4 41.4 all-gather.10
  147.0 41.9 all-gather.12
  191.4 73.6 reduce-scatter.2
  267.5 73.9 reduce-scatter.4
